TPU v7x, 256 devices: a whole 4x4x8 slice. The times are simulated.
256 devices in a mesh: dp: 32 (over z, x), cent: 8 (over y, core).
Axes of the slice: x: 4, y: 4, z: 8, core: 2. Of those that a mesh axis runs over, the one named last changes fastest.
Arguments:
- token_embeds: bfloat16 [32768, 128], P(('dp', 'cent')), may hold values from -60 to 60
- centroids: bfloat16 [65536, 128], P('cent'), may hold values from -20 to 20
- targets: int32 [32768], P(('dp', 'cent')), may hold values from 0 to 65535
- token_weights: bfloat16 [32768], P(('dp', 'cent')), may hold values from 1 to 8
Outputs:
- grad_tokens: float32 [32768, 128], P(('dp', 'cent'))
- grad_centroids: float32 [65536, 128], P('cent')
All inputs are finite; a program needn't handle non-finite values.
Results may differ from a plain program's by a relative error of at most 0.00058.
Values may be sent and summed in bfloat16 or wider, within the bound.
No kernel may reach another device: no remote copies, remote signals or barrier semaphores. Data moves between devices by JAX's collectives and lax.ppermute only.
A program may use at most 64 MiB of HBM per device.

v0:
```python
import math

import jax
import jax.numpy as jnp
from jax import lax
from jax.experimental import pallas as pl
from jax.experimental.pallas import tpu as pltpu
from jax.sharding import PartitionSpec as P

SCALE = 1.0 / math.sqrt(128.0)
RATE = math.log2(math.e) / math.sqrt(128.0)
F32 = jnp.float32
BF16 = jnp.bfloat16
TOP = 32700.0
STEPS = 32.0
VM = pl.BlockSpec(memory_space=pltpu.VMEM)
SM = pl.BlockSpec(memory_space=pltpu.SMEM)
RING = (0, 1, 3, 2)


def dot(a, b, ca, cb):
    return lax.dot_general(a, b, (((ca,), (cb,)), ((), ())), preferred_element_type=F32)


def params(mib):
    return pltpu.CompilerParams(vmem_limit_bytes=mib * 2**20)


def cost(flops, transcendentals=0):
    return pl.CostEstimate(flops=flops, bytes_accessed=2**21, transcendentals=transcendentals)


def encode(x):
    largest = jnp.max(jnp.abs(x), axis=0, keepdims=True)
    k = jnp.ceil(jnp.log2(jnp.maximum(largest, 1e-35)) * STEPS)
    q = jnp.round(x * (jnp.exp2(k * (-1.0 / STEPS)) * TOP))
    return q.astype(jnp.int32).astype(jnp.int16), k.astype(jnp.int32).astype(jnp.int16)


def scale_of(k):
    return jnp.exp2(k.astype(F32) * (1.0 / STEPS)) * (1.0 / TOP)


def pass_one_kernel(rows, e_ref, c_ref, info_ref, out_ref, la, lb):
    T = 1024
    n = c_ref.shape[0] // rows

    def fill(i, dst, m):
        c = c_ref[pl.ds(pl.multiple_of(i * rows, rows), rows), :]
        l = dot(c, e_ref[...], 1, 1)
        dst[...] = l
        return jnp.maximum(m, jnp.max(l.reshape(rows // 8, 8, T), axis=0))

    def add(src, s, m_of_s, m):
        l = src[...].reshape(rows // 8, 8, T)
        return s * jnp.exp2((m_of_s - m) * RATE) + jnp.sum(jnp.exp2((l - m[None]) * RATE), axis=0)

    m_old = jnp.full((8, T), -3.0e38, F32)
    s = jnp.zeros((8, T), F32)
    m = fill(0, la, m_old)

    def body(k, state):
        m_old, m, s = state
        m_b = fill(2 * k + 1, lb, m)
        s = add(la, s, m_old, m)
        m_a = fill(2 * k + 2, la, m_b)
        s = add(lb, s, m, m_b)
        return m_b, m_a, s

    m_old, m, s = lax.fori_loop(0, n // 2 - 1, body, (m_old, m, s))
    m_b = fill(n - 1, lb, m)
    s = add(la, s, m_old, m)
    s = add(lb, s, m, m_b)
    m = m_b
    peak = jnp.max(m, axis=0, keepdims=True)
    total = jnp.sum(s * jnp.exp2((m - peak) * RATE), axis=0, keepdims=True)
    cut = [slice(j * 128, (j + 1) * 128) for j in range(8)]
    stats = jnp.concatenate([peak[:, c] for c in cut] + [total[:, c] for c in cut], axis=0)
    for i in range(32):
        out_ref[i, 0:16, :] = stats
        out_ref[i, 16:24, :] = info_ref[...]


def pass_one(e, c, info, rows=1024):
    return pl.pallas_call(
        lambda *r: pass_one_kernel(rows, *r),
        in_specs=[VM, VM, VM],
        out_specs=VM,
        out_shape=jax.ShapeDtypeStruct((32, 24, 128), F32),
        scratch_shapes=[
            pltpu.VMEM((rows, 1024), F32),
            pltpu.VMEM((rows, 1024), F32),
        ],
        compiler_params=params(24),
        cost_estimate=cost(8 * 2**30, 2**23),
        name="pass_one",
    )(e, c, info)


def combine(x_ref, x):
    parts = [x_ref[x * 8 + i] for i in range(8)]
    m = parts[0][0:8]
    for v in parts[1:]:
        m = jnp.maximum(m, v[0:8])
    s = sum(v[8:16] * jnp.exp2((v[0:8] - m) * RATE) for v in parts)
    w = jnp.concatenate([v[16:17] for v in parts], axis=0)
    g = jnp.concatenate([v[17:18] for v in parts], axis=0)
    return m, w / s, w, g


def token_kernel(rows, base_ref, e_ref, st_ref, c_ref, out_ref, M, R, W, G, acc, la, lb, sa, sb):
    T = 1024
    n = c_ref.shape[0] // rows
    sub = lax.broadcasted_iota(jnp.int32, (8, 128), 0)
    m, r, w, g = combine(st_ref, base_ref[2])
    for j in range(8):
        sl = slice(j * 128, (j + 1) * 128)
        M[:, sl] = jnp.broadcast_to(m[j : j + 1], (8, 128))
        R[:, sl] = jnp.broadcast_to(r[j : j + 1], (8, 128))
        W[:, sl] = jnp.broadcast_to(w[j : j + 1], (8, 128))
        G[:, sl] = jnp.broadcast_to(g[j : j + 1], (8, 128)).astype(jnp.int32) - sub - base_ref[0]
    acc[...] = jnp.zeros_like(acc)

    def at(i):
        return pl.ds(pl.multiple_of(i * rows, rows), rows)

    def fill(i, dst):
        dst[...] = dot(c_ref[at(i), :], e_ref[...], 1, 1)

    def slope(i, src, dst):
        l = src[...].reshape(rows // 8, 8, T)
        p = jnp.exp2((l - M[...][None]) * RATE) * R[...][None]
        k8 = lax.broadcasted_iota(jnp.int32, (rows // 8, 8, T), 0) * 8
        p = p - jnp.where((G[...] - i * rows)[None] == k8, W[...][None], 0.0)
        dst[...] = p.reshape(rows, T).astype(BF16)

    def add(i, src):
        acc[...] += dot(c_ref[at(i), :], src[...], 0, 0)

    fill(0, la)
    fill(1, lb)
    slope(0, la, sa)

    def body(k, _):
        fill(2 * k + 2, la)
        slope(2 * k + 1, lb, sb)
        add(2 * k, sa)
        fill(2 * k + 3, lb)
        slope(2 * k + 2, la, sa)
        add(2 * k + 1, sb)
        return 0

    lax.fori_loop(0, n // 2 - 1, body, 0)
    slope(n - 1, lb, sb)
    add(n - 2, sa)
    add(n - 1, sb)
    for j in range(8):
        q, k = encode(acc[:, j * 128 : (j + 1) * 128])
        out_ref[j, 0:128, :] = q
        out_ref[j, 128:144, :] = jnp.broadcast_to(k, (16, 128))


def token_grads(base, e, st, c, rows=2048):
    return pl.pallas_call(
        lambda *r: token_kernel(rows, *r),
        in_specs=[SM, VM, VM, VM],
        out_specs=VM,
        out_shape=jax.ShapeDtypeStruct((8, 144, 128), jnp.int16),
        scratch_shapes=[
        ]
        + [pltpu.VMEM((8, 1024), F32)] * 3
        + [pltpu.VMEM((8, 1024), jnp.int32), pltpu.VMEM((128, 1024), F32)]
        + [pltpu.VMEM((rows, 1024), F32)] * 2
        + [pltpu.VMEM((rows, 1024), BF16)] * 2,
        compiler_params=params(40),
        cost_estimate=cost(12 * 2**30, 2**23),
        name="token_grads",
    )(base, e, st, c)


def centroid_kernel(T, base_ref, e0, e1, e2, e3, st_ref, c_ref, out_ref, E, ET, ST, acc, la, lb, sa, sb):
    N = 2048
    n = 4096 // T
    c = c_ref[pl.ds(pl.multiple_of(base_ref[1], N), N), :]
    la[...] = dot(e0[...], c, 1, 1)
    for x, e in enumerate((e0, e1, e2, e3)):
        E[x * 1024 : (x + 1) * 1024, :] = e[...]
    for x, step in enumerate((0, 3, 1, 2)):
        stats = combine(st_ref, lax.rem(base_ref[2] + step, 4))
        for j in range(8):
            b = x * 8 + j
            tile = jnp.concatenate([v[j : j + 1] for v in stats] + [jnp.zeros((4, 128), F32)], axis=0)
            ST[b * 128 : (b + 1) * 128, :] = tile.T
        ET[:, x * 1024 : (x + 1) * 1024] = E[x * 1024 : (x + 1) * 1024, :].T
    acc[...] = jnp.zeros_like(acc)
    base = base_ref[0] + base_ref[1]

    def at(i):
        return pl.ds(pl.multiple_of(i * T, T), T)

    def fill(i, dst):
        dst[...] = dot(E[at(i), :], c, 1, 1)

    def slope(i, src, dst):
        st = ST[at(i), :]
        p = jnp.exp2((src[...] - st[:, 0:1]) * RATE) * st[:, 1:2]
        place = lax.broadcasted_iota(jnp.int32, (T, N), 1)
        hit = (st[:, 3:4].astype(jnp.int32) - base) == place
        dst[...] = (p - jnp.where(hit, st[:, 2:3], 0.0)).astype(BF16)

    def add(i, src):
        acc[...] += dot(ET[:, at(i)], src[...], 1, 0)

    fill(1, lb)
    slope(0, la, sa)

    def body(k, _):
        fill(2 * k + 2, la)
        slope(2 * k + 1, lb, sb)
        add(2 * k, sa)
        fill(2 * k + 3, lb)
        slope(2 * k + 2, la, sa)
        add(2 * k + 1, sb)
        return 0

    lax.fori_loop(0, n // 2 - 1, body, 0)
    slope(n - 1, lb, sb)
    add(n - 2, sa)
    add(n - 1, sb)
    for z in range(8):
        q, k = encode(acc[:, z * 256 : (z + 1) * 256])
        out_ref[z, 0:128, :] = q
        out_ref[z, 128:144, :] = jnp.broadcast_to(k, (16, 256))


def centroid_grads(base, es, st, c, T=1024):
    return pl.pallas_call(
        lambda *r: centroid_kernel(T, *r),
        in_specs=[pl.BlockSpec(memory_space=pltpu.SMEM)] + [VM] * 6,
        out_specs=VM,
        out_shape=jax.ShapeDtypeStruct((8, 144, 256), jnp.int16),
        scratch_shapes=[
            pltpu.VMEM((4096, 128), BF16),
            pltpu.VMEM((128, 4096), BF16),
            pltpu.VMEM((4096, 8), F32),
            pltpu.VMEM((128, 2048), F32),
            pltpu.VMEM((T, 2048), F32),
            pltpu.VMEM((T, 2048), F32),
            pltpu.VMEM((T, 2048), BF16),
            pltpu.VMEM((T, 2048), BF16),
        ],
        compiler_params=params(48),
        cost_estimate=cost(12 * 2**30, 2**23),
        name="centroid_grads",
    )(base, *es, st, c)


def total_of(parts):
    total = None
    for ref in parts:
        part = ref[0:128, :].astype(F32) * scale_of(ref[128:144, :])[0:1]
        total = part if total is None else total + part
    return total.T * SCALE


def sum_tokens_kernel(*refs):
    refs[8][...] = total_of(refs[:8])


def sum_tokens(r):
    return pl.pallas_call(
        sum_tokens_kernel,
        in_specs=[VM] * 8,
        out_specs=VM,
        out_shape=jax.ShapeDtypeStruct((128, 128), F32),
        cost_estimate=cost(2**18),
        name="sum_tokens",
    )(*r)


def sum_kernel(in_ref, out_ref):
    q, k = encode(total_of([in_ref.at[z] for z in range(8)]))
    block = jnp.concatenate([q, jnp.broadcast_to(k, (16, 128))], axis=0)
    for z in range(8):
        out_ref[z] = block


def sum_planes(r):
    return pl.pallas_call(
        sum_kernel,
        in_specs=[VM],
        out_specs=VM,
        out_shape=jax.ShapeDtypeStruct((8, 272, 128), jnp.int16),
        cost_estimate=cost(2**22),
        name="sum_planes",
    )(r)


def widen(r):
    return r[:, 0:256, :].astype(F32) * scale_of(r[:, 256:257, :])


def shift(x, axis, k):
    return lax.ppermute(x, axis, [(i, (i + k) % 4) for i in range(4)])


def ring(x, axis):
    return [x] + [shift(x, axis, k) for k in RING[1:]]


def exchange(x, me, steps):
    blocks = [lax.dynamic_index_in_dim(x, me ^ k, 0, keepdims=False) for k in steps]
    return [
        lax.ppermute(b, ("y", "c"), [(i, i ^ k) for i in range(8)]) if k else b
        for b, k in zip(blocks, steps)
    ]


def local(token_embeds, centroids, targets, token_weights):
    info = jnp.stack([token_weights.astype(F32), targets.astype(F32)])
    info = jnp.concatenate([info, jnp.zeros((6, 128), F32)], axis=0)
    x, y, core = lax.axis_index("x"), lax.axis_index("y"), lax.axis_index("c")
    cent = y * 2 + core
    base = jnp.stack([cent * 8192, x * 2048, x, y]).astype(jnp.int32)
    pair = lax.all_gather(token_embeds, "c", axis=0, tiled=True)
    spread = jnp.broadcast_to(pair[None], (4, 256, 128))
    group = lax.all_to_all(spread, "y", 0, 0, tiled=True).reshape(1024, 128)
    plane = ring(group, "x")
    stats = pass_one(group, centroids, info)
    stats, *plane = lax.optimization_barrier((stats, *plane))
    stats = lax.all_to_all(stats, ("x", "y", "c"), 0, 0, tiled=True)
    codes = centroid_grads(base, plane, stats, centroids)
    codes = lax.all_to_all(codes, "z", 0, 0, tiled=True)
    token_codes = token_grads(base, group, stats, centroids)
    early = exchange(token_codes, cent, (0, 1, 4))
    codes, *early = lax.optimization_barrier((codes, *early))
    codes = sum_planes(codes)
    codes, token_codes = lax.optimization_barrier((codes, token_codes))
    parts = early + exchange(token_codes, cent, (2, 3, 5, 6, 7))
    codes = lax.all_to_all(codes, "z", 0, 0, tiled=True)
    codes = lax.all_gather(codes, "x", axis=0, tiled=True)
    return sum_tokens(parts), widen(codes).reshape(8192, 128)


def solution(mesh):
    torus = jax.sharding.Mesh(mesh.devices.reshape(8, 4, 4, 2), ("z", "x", "y", "c"))
    tokens = P(("z", "x", "y", "c"))
    return jax.shard_map(
        local,
        mesh=torus,
        in_specs=(P(("z", "x", "y", "c"), None), P(("y", "c"), None), tokens, tokens),
        out_specs=(P(("z", "x", "y", "c"), None), P(("y", "c"), None)),
        check_vma=False,
    )
```

profile of v0, /device:TPU:1, one launch (start us, length us, event | category | flops | bytes accessed | tf_op | source)
XLA Modules:
  0.0 135.8 jit_solution(16932410789756986110)
XLA Ops:
  0.6 5.0 %all_gather.6 = bf16[256,128]{1,0:T(8,128)(2,1)S(1)} all-gather(bf16[128,128]{1,0:T(8,128)(2,1)} %param.4), channel_id=1, replica_groups=mesh['z'=8,'x'=4,'y'=4,'c'=2] {'c'}, dimensions={0}, use_global_device_ids=true | all-gather | bytes 98304 | tf_op jit(solution)/shard_map/all_gather | solution.py:325
  6.3 3.4 %all-to-all-start = ((bf16[4,256,128]{2,1,0:T(8,128)(2,1)}), bf16[4,256,128]{2,1,0:T(8,128)(2,1)S(1)}, u32[]{:S(2)}, u32[]{:S(2)}) async-start(bf16[4,256,128]{2,1,0:T(8,128)(2,1)} %broadcast_in_dim.4), calls=%async_computation | async-start | bytes 524288 | tf_op jit(solution)/shard_map/all_to_all | solution.py:327
  11.2 4.6 %all-to-all-done = bf16[4,256,128]{2,1,0:T(8,128)(2,1)S(1)} async-done(((bf16[4,256,128]{2,1,0:T(8,128)(2,1)}), bf16[4,256,128]{2,1,0:T(8,128)(2,1)S(1)}, u32[]{:S(2)}, u32[]{:S(2)}) %all-to-all-start) | async-done | bytes 262176 | tf_op jit(solution)/shard_map/all_to_all | solution.py:327
  15.9 1.5 %collective-permute-start.2 = (bf16[1024,128]{1,0:T(8,128)(2,1)S(1)}, bf16[1024,128]{1,0:T(8,128)(2,1)S(1)}, u32[]{:S(2)}, u32[]{:S(2)}) collective-permute-start(bf16[1024,128]{1,0:T(8,128)(2,1)S(1)} %bitcast.29), channel_id=1, source_target_pairs={{0,16},{8,24},{16,0},{24,8},{1,17},{9,25},{17,1},{25,9},{2,18},{10... | collective-permute-start | bytes 786440 | tf_op jit(solution)/shard_map/ppermute | solution.py:304
  18.8 1.6 %copy-done = bf16[8192,128]{1,0:T(8,128)(2,1)S(1)} copy-done((bf16[8192,128]{1,0:T(8,128)(2,1)S(1)}, bf16[8192,128]{1,0:T(8,128)(2,1)}, u32[]{:S(2)}) %copy-start) | copy-done | bytes 2097176
  20.4 9.0 %pass_one.1 = f32[32,24,128]{2,1,0:T(8,128)} custom-call(bf16[1024,128]{1,0:T(8,128)(2,1)S(1)} %bitcast.32, bf16[8192,128]{1,0:T(8,128)(2,1)S(1)} %copy-done, f32[8,128]{1,0:T(8,128)S(1)} %maximum_maximum_fusion.r_2_), custom_call_target="tpu_custom_call" | custom-call | flops 8589934592 | bytes 2097152 | tf_op jit(solution)/shard_map/pass_one/pallas_call | solution.py:85
  31.3 6.0 %all-to-all-start.1 = ((f32[32,24,128]{2,1,0:T(8,128)}), f32[32,24,128]{2,1,0:T(8,128)S(1)}, u32[]{:S(2)}, u32[]{:S(2)}) async-start(f32[32,24,128]{2,1,0:T(8,128)} %pass_one.1), calls=%async_computation.1 | async-start | bytes 786432 | tf_op jit(solution)/shard_map/all_to_all | solution.py:331
  37.5 10.0 %all-to-all-done.1.r_5_.r_2_ = f32[32,24,128]{2,1,0:T(8,128)S(1)} async-done(((f32[32,24,128]{2,1,0:T(8,128)}), f32[32,24,128]{2,1,0:T(8,128)S(1)}, u32[]{:S(2)}, u32[]{:S(2)}) %all-to-all-start.1) | async-done | bytes 393248 | tf_op jit(solution)/shard_map/all_to_all | solution.py:331
  48.4 15.1 %centroid_grads.1 = s16[8,144,256]{2,1,0:T(8,128)(2,1)} custom-call(s32[4]{0:T(128)S(1)} %pad_add_fusion.r_0_, bf16[1024,128]{1,0:T(8,128)(2,1)S(1)} %bitcast.33, bf16[1024,128]{1,0:T(8,128)(2,1)S(1)} %copy-done.3, bf16[1024,128]{1,0:T(8,128)(2,1)S(1)} %collective-permute-done.1.r_3_, bf16[1024,128]{1,0:T(8,128)(2,1)S(1)} %collective-permute-done.2.r_4_, ...), custom_call_target="tpu_custom_call" | custom-call | flops 12884901888 | bytes 2097152 | tf_op jit(solution)/shard_map/centroid_grads/pallas_call | solution.py:237
  63.5 8.2 %all-to-all-start.2 = ((s16[8,144,256]{2,1,0:T(8,128)(2,1)}), s16[8,144,256]{2,1,0:T(8,128)(2,1)}, u32[]{:S(2)}, u32[]{:S(2)}) async-start(s16[8,144,256]{2,1,0:T(8,128)(2,1)} %centroid_grads.1), calls=%async_computation.2 | async-start | bytes 1179648 | tf_op jit(solution)/shard_map/all_to_all | solution.py:333
  71.7 11.5 %token_grads.1 = s16[8,144,128]{2,1,0:T(8,128)(2,1)S(1)} custom-call(s32[4]{0:T(128)S(1)} %pad_add_fusion.r_0_, bf16[1024,128]{1,0:T(8,128)(2,1)S(1)} %bitcast.34, f32[32,24,128]{2,1,0:T(8,128)S(1)} %all-to-all-done.1.r_5_.r_2_, bf16[8192,128]{1,0:T(8,128)(2,1)S(1)} %copy-done.1), custom_call_target="tpu_custom_call" | custom-call | flops 12884901888 | bytes 2097152 | tf_op jit(solution)/shard_map/token_grads/pallas_call | solution.py:164
  84.3 1.4 %collective-permute-start.3 = (s16[144,128]{1,0:T(8,128)(2,1)S(1)}, s16[144,128]{1,0:T(8,128)(2,1)S(1)}, u32[]{:S(2)}, u32[]{:S(2)}) collective-permute-start(s16[144,128]{1,0:T(8,128)(2,1)S(1)} %get-tuple-element.30), channel_id=1, source_target_pairs={{0,1},{1,0},{2,3},{3,2},{4,5},{5,4},{6,7},{7,6},{8,9},{9,8},{10,11... | collective-permute-start | bytes 110600 | tf_op jit(solution)/shard_map/ppermute | solution.py:314
  85.7 2.9 %collective-permute-done.4.refs_2_ = s16[144,128]{1,0:T(8,128)(2,1)S(1)} collective-permute-done((s16[144,128]{1,0:T(8,128)(2,1)S(1)}, s16[144,128]{1,0:T(8,128)(2,1)S(1)}, u32[]{:S(2)}, u32[]{:S(2)}) %collective-permute-start.4) | collective-permute-done | bytes 36896 | tf_op jit(solution)/shard_map/ppermute | solution.py:314
  88.6 2.6 %all-to-all-done.2.in_ref = s16[8,144,256]{2,1,0:T(8,128)(2,1)} async-done(((s16[8,144,256]{2,1,0:T(8,128)(2,1)}), s16[8,144,256]{2,1,0:T(8,128)(2,1)}, u32[]{:S(2)}, u32[]{:S(2)}) %all-to-all-start.2) | async-done | bytes 589856 | tf_op jit(solution)/shard_map/all_to_all | solution.py:333
  91.2 2.2 %sum_planes.1 = s16[8,272,128]{2,1,0:T(8,128)(2,1)} custom-call(s16[8,144,256]{2,1,0:T(8,128)(2,1)} %all-to-all-done.2.in_ref), custom_call_target="tpu_custom_call" | custom-call | flops 4194304 | bytes 2097152 | tf_op jit(solution)/shard_map/sum_planes/pallas_call | solution.py:289
  93.4 3.6 %all-to-all-start.3 = ((s16[8,272,128]{2,1,0:T(8,128)(2,1)}), s16[8,272,128]{2,1,0:T(8,128)(2,1)S(1)}, u32[]{:S(2)}, u32[]{:S(2)}) async-start(s16[8,272,128]{2,1,0:T(8,128)(2,1)} %sum_planes.1), calls=%async_computation.3 | async-start | bytes 1114112 | tf_op jit(solution)/shard_map/all_to_all | solution.py:340
  97.1 2.9 %collective-permute-start.9 = (s16[144,128]{1,0:T(8,128)(2,1)S(1)}, s16[144,128]{1,0:T(8,128)(2,1)S(1)}, u32[]{:S(2)}, u32[]{:S(2)}) collective-permute-start(s16[144,128]{1,0:T(8,128)(2,1)S(1)} %get-tuple-element.24), channel_id=1, source_target_pairs={{0,7},{1,6},{2,5},{3,4},{4,3},{5,2},{6,1},{7,0},{8,15},{9,14},{10,... | collective-permute-start | bytes 110600 | tf_op jit(solution)/shard_map/ppermute | solution.py:314
  100.0 1.6 %collective-permute-start.8 = (s16[144,128]{1,0:T(8,128)(2,1)S(1)}, s16[144,128]{1,0:T(8,128)(2,1)S(1)}, u32[]{:S(2)}, u32[]{:S(2)}) collective-permute-start(s16[144,128]{1,0:T(8,128)(2,1)S(1)} %get-tuple-element.25), channel_id=1, source_target_pairs={{0,6},{1,7},{2,4},{3,5},{4,2},{5,3},{6,0},{7,1},{8,14},{9,15},{10,... | collective-permute-start | bytes 110600 | tf_op jit(solution)/shard_map/ppermute | solution.py:314
  101.6 1.9 %collective-permute-start.6 = (s16[144,128]{1,0:T(8,128)(2,1)S(1)}, s16[144,128]{1,0:T(8,128)(2,1)S(1)}, u32[]{:S(2)}, u32[]{:S(2)}) collective-permute-start(s16[144,128]{1,0:T(8,128)(2,1)S(1)} %get-tuple-element.27), channel_id=1, source_target_pairs={{0,3},{1,2},{2,1},{3,0},{4,7},{5,6},{6,5},{7,4},{8,11},{9,10},{10,... | collective-permute-start | bytes 110600 | tf_op jit(solution)/shard_map/ppermute | solution.py:314
  104.0 2.8 %collective-permute-done.7.refs_5_ = s16[144,128]{1,0:T(8,128)(2,1)S(1)} collective-permute-done((s16[144,128]{1,0:T(8,128)(2,1)S(1)}, s16[144,128]{1,0:T(8,128)(2,1)S(1)}, u32[]{:S(2)}, u32[]{:S(2)}) %collective-permute-start.7) | collective-permute-done | bytes 36896 | tf_op jit(solution)/shard_map/ppermute | solution.py:314
  108.0 1.7 %sum_tokens.1 = f32[128,128]{1,0:T(8,128)} custom-call(s16[144,128]{1,0:T(8,128)(2,1)} %get-tuple-element.18.refs_0_, s16[144,128]{1,0:T(8,128)(2,1)} %copy-done.5, s16[144,128]{1,0:T(8,128)(2,1)} %copy-done.4, s16[144,128]{1,0:T(8,128)(2,1)} %copy-done.10, s16[144,128]{1,0:T(8,128)(2,1)} %copy-done.9, s16[144,128]{1,0:T(8,128)(2,1)} %copy-done.8, ...), custom_call_target="tpu_custom_call" | custom-call | flops 262144 | bytes 2097152 | tf_op jit(solution)/shard_map/sum_tokens/pallas_call | solution.py:271
  109.7 4.0 %all-to-all-done.3 = s16[8,272,128]{2,1,0:T(8,128)(2,1)S(1)} async-done(((s16[8,272,128]{2,1,0:T(8,128)(2,1)}), s16[8,272,128]{2,1,0:T(8,128)(2,1)S(1)}, u32[]{:S(2)}, u32[]{:S(2)}) %all-to-all-start.3) | async-done | bytes 557088 | tf_op jit(solution)/shard_map/all_to_all | solution.py:340
  113.7 19.4 %all-gather.1 = s16[32,272,128]{2,1,0:T(8,128)(2,1)S(1)} all-gather(s16[8,272,128]{2,1,0:T(8,128)(2,1)S(1)} %all-to-all-done.3), channel_id=1, replica_groups=mesh['z'=8,'x'=4,'y'=4,'c'=2] {'x'}, dimensions={0}, use_global_device_ids=true | all-gather | bytes 2785280 | tf_op jit(solution)/shard_map/all_gather | solution.py:341
  133.1 2.7 %convert_multiply_fusion = f32[32,256,128]{2,1,0:T(8,128)} fusion(s16[32,272,128]{2,1,0:T(8,128)(2,1)S(1)} %all-gather.1, f32[32,128]{1,0:T(8,128)S(1)} %multiply_bitcast_fusion), kind=kLoop, calls=%fused_computation | loop fusion | flops 2097152 | bytes 6307840 | tf_op jit(solution)/shard_map/mul | solution.py:300
  (45 shorter events, 9.4 us)
Async XLA Ops:
  6.3 9.5 %all-to-all-start = ((bf16[4,256,128]{2,1,0:T(8,128)(2,1)}), bf16[4,256,128]{2,1,0:T(8,128)(2,1)S(1)}, u32[]{:S(2)}, u32[]{:S(2)}) async-start(bf16[4,256,128]{2,1,0:T(8,128)(2,1)} %broadcast_in_dim.4), calls=%async_computation | async-start | bytes 524288 | tf_op jit(solution)/shard_map/all_to_all | solution.py:327
  15.9 13.6 %collective-permute-start.2 = (bf16[1024,128]{1,0:T(8,128)(2,1)S(1)}, bf16[1024,128]{1,0:T(8,128)(2,1)S(1)}, u32[]{:S(2)}, u32[]{:S(2)}) collective-permute-start(bf16[1024,128]{1,0:T(8,128)(2,1)S(1)} %bitcast.29), channel_id=1, source_target_pairs={{0,16},{8,24},{16,0},{24,8},{1,17},{9,25},{17,1},{25,9},{2,18},{10... | collective-permute-start | bytes 786440 | tf_op jit(solution)/shard_map/ppermute | solution.py:304
  17.3 12.1 %collective-permute-start.1 = (bf16[1024,128]{1,0:T(8,128)(2,1)S(1)}, bf16[1024,128]{1,0:T(8,128)(2,1)S(1)}, u32[]{:S(2)}, u32[]{:S(2)}) collective-permute-start(bf16[1024,128]{1,0:T(8,128)(2,1)S(1)} %bitcast.30), channel_id=1, source_target_pairs={{0,24},{8,0},{16,8},{24,16},{1,25},{9,1},{17,9},{25,17},{2,26},{10... | collective-permute-start | bytes 786440 | tf_op jit(solution)/shard_map/ppermute | solution.py:304
  18.2 12.4 %collective-permute-start = (bf16[1024,128]{1,0:T(8,128)(2,1)S(1)}, bf16[1024,128]{1,0:T(8,128)(2,1)S(1)}, u32[]{:S(2)}, u32[]{:S(2)}) collective-permute-start(bf16[1024,128]{1,0:T(8,128)(2,1)S(1)} %bitcast.31), channel_id=1, source_target_pairs={{0,8},{8,16},{16,24},{24,0},{1,9},{9,17},{17,25},{25,1},{2,10},{10... | collective-permute-start | bytes 786440 | tf_op jit(solution)/shard_map/ppermute | solution.py:304
  18.8 1.6 %copy-start = (bf16[8192,128]{1,0:T(8,128)(2,1)S(1)}, bf16[8192,128]{1,0:T(8,128)(2,1)}, u32[]{:S(2)}) copy-start(bf16[8192,128]{1,0:T(8,128)(2,1)} %r_3_.1) | copy-start | bytes 6291460
  20.4 27.1 %copy-start.1 = (bf16[8192,128]{1,0:T(8,128)(2,1)S(1)}, bf16[8192,128]{1,0:T(8,128)(2,1)}, u32[]{:S(2)}) copy-start(bf16[8192,128]{1,0:T(8,128)(2,1)} %r_3_.1) | copy-start | bytes 6291460
  30.6 0.7 copy-start.2
  31.3 16.2 %all-to-all-start.1 = ((f32[32,24,128]{2,1,0:T(8,128)}), f32[32,24,128]{2,1,0:T(8,128)S(1)}, u32[]{:S(2)}, u32[]{:S(2)}) async-start(f32[32,24,128]{2,1,0:T(8,128)} %pass_one.1), calls=%async_computation.1 | async-start | bytes 786432 | tf_op jit(solution)/shard_map/all_to_all | solution.py:331
  47.5 1.0 copy-start.3
  63.5 27.7 %all-to-all-start.2 = ((s16[8,144,256]{2,1,0:T(8,128)(2,1)}), s16[8,144,256]{2,1,0:T(8,128)(2,1)}, u32[]{:S(2)}, u32[]{:S(2)}) async-start(s16[8,144,256]{2,1,0:T(8,128)(2,1)} %centroid_grads.1), calls=%async_computation.2 | async-start | bytes 1179648 | tf_op jit(solution)/shard_map/all_to_all | solution.py:333
  83.9 4.7 %collective-permute-start.4 = (s16[144,128]{1,0:T(8,128)(2,1)S(1)}, s16[144,128]{1,0:T(8,128)(2,1)S(1)}, u32[]{:S(2)}, u32[]{:S(2)}) collective-permute-start(s16[144,128]{1,0:T(8,128)(2,1)S(1)} %get-tuple-element.29), channel_id=1, source_target_pairs={{0,4},{1,5},{2,6},{3,7},{4,0},{5,1},{6,2},{7,3},{8,12},{9,13},{10,... | collective-permute-start | bytes 110600 | tf_op jit(solution)/shard_map/ppermute | solution.py:314
  84.3 4.3 %collective-permute-start.3 = (s16[144,128]{1,0:T(8,128)(2,1)S(1)}, s16[144,128]{1,0:T(8,128)(2,1)S(1)}, u32[]{:S(2)}, u32[]{:S(2)}) collective-permute-start(s16[144,128]{1,0:T(8,128)(2,1)S(1)} %get-tuple-element.30), channel_id=1, source_target_pairs={{0,1},{1,0},{2,3},{3,2},{4,5},{5,4},{6,7},{7,6},{8,9},{9,8},{10,11... | collective-permute-start | bytes 110600 | tf_op jit(solution)/shard_map/ppermute | solution.py:314
  88.6 18.3 %copy-start.4 = (s16[144,128]{1,0:T(8,128)(2,1)}, s16[144,128]{1,0:T(8,128)(2,1)S(1)}, u32[]{:S(2)}) copy-start(s16[144,128]{1,0:T(8,128)(2,1)S(1)} %collective-permute-done.4.refs_2_) | copy-start | bytes 110596
  88.6 18.3 %copy-start.5 = (s16[144,128]{1,0:T(8,128)(2,1)}, s16[144,128]{1,0:T(8,128)(2,1)S(1)}, u32[]{:S(2)}) copy-start(s16[144,128]{1,0:T(8,128)(2,1)S(1)} %collective-permute-done.3.refs_1_) | copy-start | bytes 110596
  93.4 20.2 %all-to-all-start.3 = ((s16[8,272,128]{2,1,0:T(8,128)(2,1)}), s16[8,272,128]{2,1,0:T(8,128)(2,1)S(1)}, u32[]{:S(2)}, u32[]{:S(2)}) async-start(s16[8,272,128]{2,1,0:T(8,128)(2,1)} %sum_planes.1), calls=%async_computation.3 | async-start | bytes 1114112 | tf_op jit(solution)/shard_map/all_to_all | solution.py:340
  97.1 6.5 %collective-permute-start.9 = (s16[144,128]{1,0:T(8,128)(2,1)S(1)}, s16[144,128]{1,0:T(8,128)(2,1)S(1)}, u32[]{:S(2)}, u32[]{:S(2)}) collective-permute-start(s16[144,128]{1,0:T(8,128)(2,1)S(1)} %get-tuple-element.24), channel_id=1, source_target_pairs={{0,7},{1,6},{2,5},{3,4},{4,3},{5,2},{6,1},{7,0},{8,15},{9,14},{10,... | collective-permute-start | bytes 110600 | tf_op jit(solution)/shard_map/ppermute | solution.py:314
  100.0 4.0 %collective-permute-start.8 = (s16[144,128]{1,0:T(8,128)(2,1)S(1)}, s16[144,128]{1,0:T(8,128)(2,1)S(1)}, u32[]{:S(2)}, u32[]{:S(2)}) collective-permute-start(s16[144,128]{1,0:T(8,128)(2,1)S(1)} %get-tuple-element.25), channel_id=1, source_target_pairs={{0,6},{1,7},{2,4},{3,5},{4,2},{5,3},{6,0},{7,1},{8,14},{9,15},{10,... | collective-permute-start | bytes 110600 | tf_op jit(solution)/shard_map/ppermute | solution.py:314
  101.6 5.2 %collective-permute-start.7 = (s16[144,128]{1,0:T(8,128)(2,1)S(1)}, s16[144,128]{1,0:T(8,128)(2,1)S(1)}, u32[]{:S(2)}, u32[]{:S(2)}) collective-permute-start(s16[144,128]{1,0:T(8,128)(2,1)S(1)} %get-tuple-element.26), channel_id=1, source_target_pairs={{0,5},{1,4},{2,7},{3,6},{4,1},{5,0},{6,3},{7,2},{8,13},{9,12},{10,... | collective-permute-start | bytes 110600 | tf_op jit(solution)/shard_map/ppermute | solution.py:314
  101.6 5.2 %collective-permute-start.6 = (s16[144,128]{1,0:T(8,128)(2,1)S(1)}, s16[144,128]{1,0:T(8,128)(2,1)S(1)}, u32[]{:S(2)}, u32[]{:S(2)}) collective-permute-start(s16[144,128]{1,0:T(8,128)(2,1)S(1)} %get-tuple-element.27), channel_id=1, source_target_pairs={{0,3},{1,2},{2,1},{3,0},{4,7},{5,6},{6,5},{7,4},{8,11},{9,10},{10,... | collective-permute-start | bytes 110600 | tf_op jit(solution)/shard_map/ppermute | solution.py:314
  103.5 3.4 %collective-permute-start.5 = (s16[144,128]{1,0:T(8,128)(2,1)S(1)}, s16[144,128]{1,0:T(8,128)(2,1)S(1)}, u32[]{:S(2)}, u32[]{:S(2)}) collective-permute-start(s16[144,128]{1,0:T(8,128)(2,1)S(1)} %get-tuple-element.28), channel_id=1, source_target_pairs={{0,2},{1,3},{2,0},{3,1},{4,6},{5,7},{6,4},{7,5},{8,10},{9,11},{10,... | collective-permute-start | bytes 110600 | tf_op jit(solution)/shard_map/ppermute | solution.py:314
  103.6 3.4 %copy-start.6 = (s16[144,128]{1,0:T(8,128)(2,1)}, s16[144,128]{1,0:T(8,128)(2,1)S(1)}, u32[]{:S(2)}) copy-start(s16[144,128]{1,0:T(8,128)(2,1)S(1)} %collective-permute-done.9.refs_7_) | copy-start | bytes 110596
  104.0 2.9 %copy-start.7 = (s16[144,128]{1,0:T(8,128)(2,1)}, s16[144,128]{1,0:T(8,128)(2,1)S(1)}, u32[]{:S(2)}) copy-start(s16[144,128]{1,0:T(8,128)(2,1)S(1)} %collective-permute-done.8.refs_6_) | copy-start | bytes 110596
  106.8 0.6 copy-start.8
  106.8 0.6 copy-start.9
  (1 other events, 0.6 us)
where the time goes:
time: 138 us; the launch traced here: 136 us
  Pallas kernels  39.5 us (29%)
  starting transfers between devices  32.5 us (24%)
  waiting for transfers between devices  28.7 us (21%)
  blocking collectives  24.3 us (18%)
  local copies, waits for them, and re-layouts  5.84 us (4%)
  other arithmetic  4.2 us (3%)
    all_gather x1, blocking collectives, local(): codes = lax.all_gather(codes, 'x', axis=0, tiled=True)  19.4 us
    pallas_call x1, Pallas kernels, centroid_grads(): pl.pallas_call(lambda *r: centroid_kernel(T, *r), in_specs=[pl.BlockSpec(...  15.1 us
    all_to_all x2, starting transfers between devices, local(): codes = lax.all_to_all(codes, 'z', 0, 0, tiled=True)  11.8 us
    pallas_call x1, Pallas kernels, token_grads(): pl.pallas_call(lambda *r: token_kernel(rows, *r), in_specs=[SM, VM, VM, V...  11.5 us
    all_to_all x1, waiting for transfers between devices, local(): stats = lax.all_to_all(stats, ('x', 'y', 'c'), 0, 0, tiled=True)  10 us
    pallas_call x1, Pallas kernels, pass_one(): pl.pallas_call(lambda *r: pass_one_kernel(rows, *r), in_specs=[VM, VM, VM...  9.01 us
    ppermute x7, starting transfers between devices, exchange(): lax.ppermute(b, ('y', 'c'), [(i, i ^ k) for i in range(8)])  8.27 us
    all_to_all x2, waiting for transfers between devices, local(): codes = lax.all_to_all(codes, 'z', 0, 0, tiled=True)  6.6 us
  transfers between devices with their start and end apart: 14, of which 9 were waited for; matrix products, arithmetic and copies ran while one was open for 2% of the time, Pallas kernels for 16%

commit v1 on v0

--- a/solution.py
+++ b/solution.py
@@ -332,11 +332,11 @@
     codes = centroid_grads(base, plane, stats, centroids)
     codes = lax.all_to_all(codes, "z", 0, 0, tiled=True)
     token_codes = token_grads(base, group, stats, centroids)
-    early = exchange(token_codes, cent, (0, 1, 4))
+    early = exchange(token_codes, cent, (0, 1, 2))
     codes, *early = lax.optimization_barrier((codes, *early))
     codes = sum_planes(codes)
     codes, token_codes = lax.optimization_barrier((codes, token_codes))
-    parts = early + exchange(token_codes, cent, (2, 3, 5, 6, 7))
+    parts = early + exchange(token_codes, cent, (3, 4, 5, 6, 7))
     codes = lax.all_to_all(codes, "z", 0, 0, tiled=True)
     codes = lax.all_gather(codes, "x", axis=0, tiled=True)
     return sum_tokens(parts), widen(codes).reshape(8192, 128)

time: 138 us -> 141 us (1.022)
  waiting for transfers between devices: 28.7 us -> 32.4 us
  blocking collectives: 24.3 us -> 26.5 us
    all_to_all x2, waiting for transfers between devices: 6.6 us -> 10.7 us  [local(): codes = lax.all_to_all(codes, 'z', 0, 0, tiled=True)]
    all_gather x1, blocking collectives: 19.4 us -> 21.5 us  [local(): codes = lax.all_gather(codes, 'x', axis=0, tiled=True)]
where the time goes in v1:
time: 141 us; the launch traced here: 140 us
  Pallas kernels  39.5 us (28%)
  waiting for transfers between devices  32.4 us (23%)
  starting transfers between devices  31.1 us (22%)
  blocking collectives  26.5 us (19%)
  local copies, waits for them, and re-layouts  5.37 us (4%)
  other arithmetic  4.2 us (3%)
    all_gather x1, blocking collectives, local(): codes = lax.all_gather(codes, 'x', axis=0, tiled=True)  21.5 us
    pallas_call x1, Pallas kernels, centroid_grads(): pl.pallas_call(lambda *r: centroid_kernel(T, *r), in_specs=[pl.BlockSpec(...  15.1 us
    all_to_all x2, starting transfers between devices, local(): codes = lax.all_to_all(codes, 'z', 0, 0, tiled=True)  11.7 us
    pallas_call x1, Pallas kernels, token_grads(): pl.pallas_call(lambda *r: token_kernel(rows, *r), in_specs=[SM, VM, VM, V...  11.5 us
    all_to_all x2, waiting for transfers between devices, local(): codes = lax.all_to_all(codes, 'z', 0, 0, tiled=True)  10.7 us
    all_to_all x1, waiting for transfers between devices, local(): stats = lax.all_to_all(stats, ('x', 'y', 'c'), 0, 0, tiled=True)  10 us
    pallas_call x1, Pallas kernels, pass_one(): pl.pallas_call(lambda *r: pass_one_kernel(rows, *r), in_specs=[VM, VM, VM...  9.01 us
    ppermute x7, starting transfers between devices, exchange(): lax.ppermute(b, ('y', 'c'), [(i, i ^ k) for i in range(8)])  6.98 us
  transfers between devices with their start and end apart: 14, of which 9 were waited for; matrix products, arithmetic and copies ran while one was open for 2% of the time, Pallas kernels for 16%

profile of v1, /device:TPU:1, one launch (start us, length us, event | category | flops | bytes accessed | tf_op | source)
XLA Modules:
  0.0 139.9 jit_solution(6896479936604965372)
XLA Ops:
  0.6 5.0 %all_gather.6 = bf16[256,128]{1,0:T(8,128)(2,1)S(1)} all-gather(bf16[128,128]{1,0:T(8,128)(2,1)} %param.4), channel_id=1, replica_groups=mesh['z'=8,'x'=4,'y'=4,'c'=2] {'c'}, dimensions={0}, use_global_device_ids=true | all-gather | bytes 98304 | tf_op jit(solution)/shard_map/all_gather | solution.py:325
  6.3 3.4 %all-to-all-start = ((bf16[4,256,128]{2,1,0:T(8,128)(2,1)}), bf16[4,256,128]{2,1,0:T(8,128)(2,1)S(1)}, u32[]{:S(2)}, u32[]{:S(2)}) async-start(bf16[4,256,128]{2,1,0:T(8,128)(2,1)} %broadcast_in_dim.4), calls=%async_computation | async-start | bytes 524288 | tf_op jit(solution)/shard_map/all_to_all | solution.py:327
  11.2 4.6 %all-to-all-done = bf16[4,256,128]{2,1,0:T(8,128)(2,1)S(1)} async-done(((bf16[4,256,128]{2,1,0:T(8,128)(2,1)}), bf16[4,256,128]{2,1,0:T(8,128)(2,1)S(1)}, u32[]{:S(2)}, u32[]{:S(2)}) %all-to-all-start) | async-done | bytes 262176 | tf_op jit(solution)/shard_map/all_to_all | solution.py:327
  15.9 1.5 %collective-permute-start.2 = (bf16[1024,128]{1,0:T(8,128)(2,1)S(1)}, bf16[1024,128]{1,0:T(8,128)(2,1)S(1)}, u32[]{:S(2)}, u32[]{:S(2)}) collective-permute-start(bf16[1024,128]{1,0:T(8,128)(2,1)S(1)} %bitcast.29), channel_id=1, source_target_pairs={{0,16},{8,24},{16,0},{24,8},{1,17},{9,25},{17,1},{25,9},{2,18},{10... | collective-permute-start | bytes 786440 | tf_op jit(solution)/shard_map/ppermute | solution.py:304
  18.8 1.6 %copy-done = bf16[8192,128]{1,0:T(8,128)(2,1)S(1)} copy-done((bf16[8192,128]{1,0:T(8,128)(2,1)S(1)}, bf16[8192,128]{1,0:T(8,128)(2,1)}, u32[]{:S(2)}) %copy-start) | copy-done | bytes 2097176
  20.4 9.0 %pass_one.1 = f32[32,24,128]{2,1,0:T(8,128)} custom-call(bf16[1024,128]{1,0:T(8,128)(2,1)S(1)} %bitcast.32, bf16[8192,128]{1,0:T(8,128)(2,1)S(1)} %copy-done, f32[8,128]{1,0:T(8,128)S(1)} %maximum_maximum_fusion.r_2_), custom_call_target="tpu_custom_call" | custom-call | flops 8589934592 | bytes 2097152 | tf_op jit(solution)/shard_map/pass_one/pallas_call | solution.py:85
  31.3 6.0 %all-to-all-start.1 = ((f32[32,24,128]{2,1,0:T(8,128)}), f32[32,24,128]{2,1,0:T(8,128)S(1)}, u32[]{:S(2)}, u32[]{:S(2)}) async-start(f32[32,24,128]{2,1,0:T(8,128)} %pass_one.1), calls=%async_computation.1 | async-start | bytes 786432 | tf_op jit(solution)/shard_map/all_to_all | solution.py:331
  37.5 10.0 %all-to-all-done.1.r_5_.r_2_ = f32[32,24,128]{2,1,0:T(8,128)S(1)} async-done(((f32[32,24,128]{2,1,0:T(8,128)}), f32[32,24,128]{2,1,0:T(8,128)S(1)}, u32[]{:S(2)}, u32[]{:S(2)}) %all-to-all-start.1) | async-done | bytes 393248 | tf_op jit(solution)/shard_map/all_to_all | solution.py:331
  48.4 15.1 %centroid_grads.1 = s16[8,144,256]{2,1,0:T(8,128)(2,1)} custom-call(s32[4]{0:T(128)S(1)} %pad_add_fusion.r_0_, bf16[1024,128]{1,0:T(8,128)(2,1)S(1)} %bitcast.33, bf16[1024,128]{1,0:T(8,128)(2,1)S(1)} %copy-done.3, bf16[1024,128]{1,0:T(8,128)(2,1)S(1)} %collective-permute-done.1.r_3_, bf16[1024,128]{1,0:T(8,128)(2,1)S(1)} %collective-permute-done.2.r_4_, ...), custom_call_target="tpu_custom_call" | custom-call | flops 12884901888 | bytes 2097152 | tf_op jit(solution)/shard_map/centroid_grads/pallas_call | solution.py:237
  63.5 8.2 %all-to-all-start.2 = ((s16[8,144,256]{2,1,0:T(8,128)(2,1)}), s16[8,144,256]{2,1,0:T(8,128)(2,1)}, u32[]{:S(2)}, u32[]{:S(2)}) async-start(s16[8,144,256]{2,1,0:T(8,128)(2,1)} %centroid_grads.1), calls=%async_computation.2 | async-start | bytes 1179648 | tf_op jit(solution)/shard_map/all_to_all | solution.py:333
  71.7 11.5 %token_grads.1 = s16[8,144,128]{2,1,0:T(8,128)(2,1)S(1)} custom-call(s32[4]{0:T(128)S(1)} %pad_add_fusion.r_0_, bf16[1024,128]{1,0:T(8,128)(2,1)S(1)} %bitcast.34, f32[32,24,128]{2,1,0:T(8,128)S(1)} %all-to-all-done.1.r_5_.r_2_, bf16[8192,128]{1,0:T(8,128)(2,1)S(1)} %copy-done.1), custom_call_target="tpu_custom_call" | custom-call | flops 12884901888 | bytes 2097152 | tf_op jit(solution)/shard_map/token_grads/pallas_call | solution.py:164
  84.6 2.1 %collective-permute-done.4.refs_2_ = s16[144,128]{1,0:T(8,128)(2,1)S(1)} collective-permute-done((s16[144,128]{1,0:T(8,128)(2,1)S(1)}, s16[144,128]{1,0:T(8,128)(2,1)S(1)}, u32[]{:S(2)}, u32[]{:S(2)}) %collective-permute-start.4) | collective-permute-done | bytes 36896 | tf_op jit(solution)/shard_map/ppermute | solution.py:314
  86.7 4.5 %all-to-all-done.2.in_ref = s16[8,144,256]{2,1,0:T(8,128)(2,1)} async-done(((s16[8,144,256]{2,1,0:T(8,128)(2,1)}), s16[8,144,256]{2,1,0:T(8,128)(2,1)}, u32[]{:S(2)}, u32[]{:S(2)}) %all-to-all-start.2) | async-done | bytes 589856 | tf_op jit(solution)/shard_map/all_to_all | solution.py:333
  91.2 2.2 %sum_planes.1 = s16[8,272,128]{2,1,0:T(8,128)(2,1)} custom-call(s16[8,144,256]{2,1,0:T(8,128)(2,1)} %all-to-all-done.2.in_ref), custom_call_target="tpu_custom_call" | custom-call | flops 4194304 | bytes 2097152 | tf_op jit(solution)/shard_map/sum_planes/pallas_call | solution.py:289
  93.4 3.5 %all-to-all-start.3 = ((s16[8,272,128]{2,1,0:T(8,128)(2,1)}), s16[8,272,128]{2,1,0:T(8,128)(2,1)S(1)}, u32[]{:S(2)}, u32[]{:S(2)}) async-start(s16[8,272,128]{2,1,0:T(8,128)(2,1)} %sum_planes.1), calls=%async_computation.3 | async-start | bytes 1114112 | tf_op jit(solution)/shard_map/all_to_all | solution.py:340
  97.0 1.5 %collective-permute-start.9 = (s16[144,128]{1,0:T(8,128)(2,1)S(1)}, s16[144,128]{1,0:T(8,128)(2,1)S(1)}, u32[]{:S(2)}, u32[]{:S(2)}) collective-permute-start(s16[144,128]{1,0:T(8,128)(2,1)S(1)} %get-tuple-element.24), channel_id=1, source_target_pairs={{0,7},{1,6},{2,5},{3,4},{4,3},{5,2},{6,1},{7,0},{8,15},{9,14},{10,... | collective-permute-start | bytes 110600 | tf_op jit(solution)/shard_map/ppermute | solution.py:314
  98.5 1.7 %collective-permute-start.8 = (s16[144,128]{1,0:T(8,128)(2,1)S(1)}, s16[144,128]{1,0:T(8,128)(2,1)S(1)}, u32[]{:S(2)}, u32[]{:S(2)}) collective-permute-start(s16[144,128]{1,0:T(8,128)(2,1)S(1)} %get-tuple-element.25), channel_id=1, source_target_pairs={{0,6},{1,7},{2,4},{3,5},{4,2},{5,3},{6,0},{7,1},{8,14},{9,15},{10,... | collective-permute-start | bytes 110600 | tf_op jit(solution)/shard_map/ppermute | solution.py:314
  100.1 3.2 %collective-permute-start.6 = (s16[144,128]{1,0:T(8,128)(2,1)S(1)}, s16[144,128]{1,0:T(8,128)(2,1)S(1)}, u32[]{:S(2)}, u32[]{:S(2)}) collective-permute-start(s16[144,128]{1,0:T(8,128)(2,1)S(1)} %get-tuple-element.27), channel_id=1, source_target_pairs={{0,4},{1,5},{2,6},{3,7},{4,0},{5,1},{6,2},{7,3},{8,12},{9,13},{10,... | collective-permute-start | bytes 110600 | tf_op jit(solution)/shard_map/ppermute | solution.py:314
  103.4 2.3 %collective-permute-done.7.refs_5_ = s16[144,128]{1,0:T(8,128)(2,1)S(1)} collective-permute-done((s16[144,128]{1,0:T(8,128)(2,1)S(1)}, s16[144,128]{1,0:T(8,128)(2,1)S(1)}, u32[]{:S(2)}, u32[]{:S(2)}) %collective-permute-start.7) | collective-permute-done | bytes 36896 | tf_op jit(solution)/shard_map/ppermute | solution.py:314
  105.9 1.3 collective-permute-done.5.refs_3_
  107.8 1.7 %sum_tokens.1 = f32[128,128]{1,0:T(8,128)} custom-call(s16[144,128]{1,0:T(8,128)(2,1)} %get-tuple-element.18.refs_0_, s16[144,128]{1,0:T(8,128)(2,1)} %copy-done.5, s16[144,128]{1,0:T(8,128)(2,1)} %copy-done.4, s16[144,128]{1,0:T(8,128)(2,1)} %copy-done.10, s16[144,128]{1,0:T(8,128)(2,1)} %copy-done.9, s16[144,128]{1,0:T(8,128)(2,1)} %copy-done.8, ...), custom_call_target="tpu_custom_call" | custom-call | flops 262144 | bytes 2097152 | tf_op jit(solution)/shard_map/sum_tokens/pallas_call | solution.py:271
  109.5 6.1 %all-to-all-done.3 = s16[8,272,128]{2,1,0:T(8,128)(2,1)S(1)} async-done(((s16[8,272,128]{2,1,0:T(8,128)(2,1)}), s16[8,272,128]{2,1,0:T(8,128)(2,1)S(1)}, u32[]{:S(2)}, u32[]{:S(2)}) %all-to-all-start.3) | async-done | bytes 557088 | tf_op jit(solution)/shard_map/all_to_all | solution.py:340
  115.6 21.5 %all-gather.1 = s16[32,272,128]{2,1,0:T(8,128)(2,1)S(1)} all-gather(s16[8,272,128]{2,1,0:T(8,128)(2,1)S(1)} %all-to-all-done.3), channel_id=1, replica_groups=mesh['z'=8,'x'=4,'y'=4,'c'=2] {'x'}, dimensions={0}, use_global_device_ids=true | all-gather | bytes 2785280 | tf_op jit(solution)/shard_map/all_gather | solution.py:341
  137.1 2.7 %convert_multiply_fusion = f32[32,256,128]{2,1,0:T(8,128)} fusion(s16[32,272,128]{2,1,0:T(8,128)(2,1)S(1)} %all-gather.1, f32[32,128]{1,0:T(8,128)S(1)} %multiply_bitcast_fusion), kind=kLoop, calls=%fused_computation | loop fusion | flops 2097152 | bytes 6307840 | tf_op jit(solution)/shard_map/mul | solution.py:300
  (45 shorter events, 8.9 us)
Async XLA Ops:
  6.3 9.5 %all-to-all-start = ((bf16[4,256,128]{2,1,0:T(8,128)(2,1)}), bf16[4,256,128]{2,1,0:T(8,128)(2,1)S(1)}, u32[]{:S(2)}, u32[]{:S(2)}) async-start(bf16[4,256,128]{2,1,0:T(8,128)(2,1)} %broadcast_in_dim.4), calls=%async_computation | async-start | bytes 524288 | tf_op jit(solution)/shard_map/all_to_all | solution.py:327
  15.9 13.6 %collective-permute-start.2 = (bf16[1024,128]{1,0:T(8,128)(2,1)S(1)}, bf16[1024,128]{1,0:T(8,128)(2,1)S(1)}, u32[]{:S(2)}, u32[]{:S(2)}) collective-permute-start(bf16[1024,128]{1,0:T(8,128)(2,1)S(1)} %bitcast.29), channel_id=1, source_target_pairs={{0,16},{8,24},{16,0},{24,8},{1,17},{9,25},{17,1},{25,9},{2,18},{10... | collective-permute-start | bytes 786440 | tf_op jit(solution)/shard_map/ppermute | solution.py:304
  17.3 12.1 %collective-permute-start.1 = (bf16[1024,128]{1,0:T(8,128)(2,1)S(1)}, bf16[1024,128]{1,0:T(8,128)(2,1)S(1)}, u32[]{:S(2)}, u32[]{:S(2)}) collective-permute-start(bf16[1024,128]{1,0:T(8,128)(2,1)S(1)} %bitcast.30), channel_id=1, source_target_pairs={{0,24},{8,0},{16,8},{24,16},{1,25},{9,1},{17,9},{25,17},{2,26},{10... | collective-permute-start | bytes 786440 | tf_op jit(solution)/shard_map/ppermute | solution.py:304
  18.2 12.4 %collective-permute-start = (bf16[1024,128]{1,0:T(8,128)(2,1)S(1)}, bf16[1024,128]{1,0:T(8,128)(2,1)S(1)}, u32[]{:S(2)}, u32[]{:S(2)}) collective-permute-start(bf16[1024,128]{1,0:T(8,128)(2,1)S(1)} %bitcast.31), channel_id=1, source_target_pairs={{0,8},{8,16},{16,24},{24,0},{1,9},{9,17},{17,25},{25,1},{2,10},{10... | collective-permute-start | bytes 786440 | tf_op jit(solution)/shard_map/ppermute | solution.py:304
  18.8 1.6 %copy-start = (bf16[8192,128]{1,0:T(8,128)(2,1)S(1)}, bf16[8192,128]{1,0:T(8,128)(2,1)}, u32[]{:S(2)}) copy-start(bf16[8192,128]{1,0:T(8,128)(2,1)} %r_3_.1) | copy-start | bytes 6291460
  20.4 27.1 %copy-start.1 = (bf16[8192,128]{1,0:T(8,128)(2,1)S(1)}, bf16[8192,128]{1,0:T(8,128)(2,1)}, u32[]{:S(2)}) copy-start(bf16[8192,128]{1,0:T(8,128)(2,1)} %r_3_.1) | copy-start | bytes 6291460
  30.6 0.7 copy-start.2
  31.3 16.2 %all-to-all-start.1 = ((f32[32,24,128]{2,1,0:T(8,128)}), f32[32,24,128]{2,1,0:T(8,128)S(1)}, u32[]{:S(2)}, u32[]{:S(2)}) async-start(f32[32,24,128]{2,1,0:T(8,128)} %pass_one.1), calls=%async_computation.1 | async-start | bytes 786432 | tf_op jit(solution)/shard_map/all_to_all | solution.py:331
  47.5 1.0 copy-start.3
  63.5 27.7 %all-to-all-start.2 = ((s16[8,144,256]{2,1,0:T(8,128)(2,1)}), s16[8,144,256]{2,1,0:T(8,128)(2,1)}, u32[]{:S(2)}, u32[]{:S(2)}) async-start(s16[8,144,256]{2,1,0:T(8,128)(2,1)} %centroid_grads.1), calls=%async_computation.2 | async-start | bytes 1179648 | tf_op jit(solution)/shard_map/all_to_all | solution.py:333
  83.9 2.8 %collective-permute-start.4 = (s16[144,128]{1,0:T(8,128)(2,1)S(1)}, s16[144,128]{1,0:T(8,128)(2,1)S(1)}, u32[]{:S(2)}, u32[]{:S(2)}) collective-permute-start(s16[144,128]{1,0:T(8,128)(2,1)S(1)} %get-tuple-element.29), channel_id=1, source_target_pairs={{0,2},{1,3},{2,0},{3,1},{4,6},{5,7},{6,4},{7,5},{8,10},{9,11},{10,... | collective-permute-start | bytes 110600 | tf_op jit(solution)/shard_map/ppermute | solution.py:314
  84.0 2.6 %collective-permute-start.3 = (s16[144,128]{1,0:T(8,128)(2,1)S(1)}, s16[144,128]{1,0:T(8,128)(2,1)S(1)}, u32[]{:S(2)}, u32[]{:S(2)}) collective-permute-start(s16[144,128]{1,0:T(8,128)(2,1)S(1)} %get-tuple-element.30), channel_id=1, source_target_pairs={{0,1},{1,0},{2,3},{3,2},{4,5},{5,4},{6,7},{7,6},{8,9},{9,8},{10,11... | collective-permute-start | bytes 110600 | tf_op jit(solution)/shard_map/ppermute | solution.py:314
  86.7 20.5 %copy-start.4 = (s16[144,128]{1,0:T(8,128)(2,1)}, s16[144,128]{1,0:T(8,128)(2,1)S(1)}, u32[]{:S(2)}) copy-start(s16[144,128]{1,0:T(8,128)(2,1)S(1)} %collective-permute-done.4.refs_2_) | copy-start | bytes 110596
  86.7 20.5 %copy-start.5 = (s16[144,128]{1,0:T(8,128)(2,1)}, s16[144,128]{1,0:T(8,128)(2,1)S(1)}, u32[]{:S(2)}) copy-start(s16[144,128]{1,0:T(8,128)(2,1)S(1)} %collective-permute-done.3.refs_1_) | copy-start | bytes 110596
  93.4 22.2 %all-to-all-start.3 = ((s16[8,272,128]{2,1,0:T(8,128)(2,1)}), s16[8,272,128]{2,1,0:T(8,128)(2,1)S(1)}, u32[]{:S(2)}, u32[]{:S(2)}) async-start(s16[8,272,128]{2,1,0:T(8,128)(2,1)} %sum_planes.1), calls=%async_computation.3 | async-start | bytes 1114112 | tf_op jit(solution)/shard_map/all_to_all | solution.py:340
  97.0 6.3 %collective-permute-start.9 = (s16[144,128]{1,0:T(8,128)(2,1)S(1)}, s16[144,128]{1,0:T(8,128)(2,1)S(1)}, u32[]{:S(2)}, u32[]{:S(2)}) collective-permute-start(s16[144,128]{1,0:T(8,128)(2,1)S(1)} %get-tuple-element.24), channel_id=1, source_target_pairs={{0,7},{1,6},{2,5},{3,4},{4,3},{5,2},{6,1},{7,0},{8,15},{9,14},{10,... | collective-permute-start | bytes 110600 | tf_op jit(solution)/shard_map/ppermute | solution.py:314
  98.5 4.9 %collective-permute-start.8 = (s16[144,128]{1,0:T(8,128)(2,1)S(1)}, s16[144,128]{1,0:T(8,128)(2,1)S(1)}, u32[]{:S(2)}, u32[]{:S(2)}) collective-permute-start(s16[144,128]{1,0:T(8,128)(2,1)S(1)} %get-tuple-element.25), channel_id=1, source_target_pairs={{0,6},{1,7},{2,4},{3,5},{4,2},{5,3},{6,0},{7,1},{8,14},{9,15},{10,... | collective-permute-start | bytes 110600 | tf_op jit(solution)/shard_map/ppermute | solution.py:314
  100.1 5.5 %collective-permute-start.7 = (s16[144,128]{1,0:T(8,128)(2,1)S(1)}, s16[144,128]{1,0:T(8,128)(2,1)S(1)}, u32[]{:S(2)}, u32[]{:S(2)}) collective-permute-start(s16[144,128]{1,0:T(8,128)(2,1)S(1)} %get-tuple-element.26), channel_id=1, source_target_pairs={{0,5},{1,4},{2,7},{3,6},{4,1},{5,0},{6,3},{7,2},{8,13},{9,12},{10,... | collective-permute-start | bytes 110600 | tf_op jit(solution)/shard_map/ppermute | solution.py:314
  100.1 5.7 %collective-permute-start.6 = (s16[144,128]{1,0:T(8,128)(2,1)S(1)}, s16[144,128]{1,0:T(8,128)(2,1)S(1)}, u32[]{:S(2)}, u32[]{:S(2)}) collective-permute-start(s16[144,128]{1,0:T(8,128)(2,1)S(1)} %get-tuple-element.27), channel_id=1, source_target_pairs={{0,4},{1,5},{2,6},{3,7},{4,0},{5,1},{6,2},{7,3},{8,12},{9,13},{10,... | collective-permute-start | bytes 110600 | tf_op jit(solution)/shard_map/ppermute | solution.py:314
  103.3 3.8 %collective-permute-start.5 = (s16[144,128]{1,0:T(8,128)(2,1)S(1)}, s16[144,128]{1,0:T(8,128)(2,1)S(1)}, u32[]{:S(2)}, u32[]{:S(2)}) collective-permute-start(s16[144,128]{1,0:T(8,128)(2,1)S(1)} %get-tuple-element.28), channel_id=1, source_target_pairs={{0,3},{1,2},{2,1},{3,0},{4,7},{5,6},{6,5},{7,4},{8,11},{9,10},{10,... | collective-permute-start | bytes 110600 | tf_op jit(solution)/shard_map/ppermute | solution.py:314
  103.3 3.8 %copy-start.6 = (s16[144,128]{1,0:T(8,128)(2,1)}, s16[144,128]{1,0:T(8,128)(2,1)S(1)}, u32[]{:S(2)}) copy-start(s16[144,128]{1,0:T(8,128)(2,1)S(1)} %collective-permute-done.9.refs_7_) | copy-start | bytes 110596
  103.4 3.8 %copy-start.7 = (s16[144,128]{1,0:T(8,128)(2,1)}, s16[144,128]{1,0:T(8,128)(2,1)S(1)}, u32[]{:S(2)}) copy-start(s16[144,128]{1,0:T(8,128)(2,1)S(1)} %collective-permute-done.8.refs_6_) | copy-start | bytes 110596
  105.6 1.6 %copy-start.8 = (s16[144,128]{1,0:T(8,128)(2,1)}, s16[144,128]{1,0:T(8,128)(2,1)S(1)}, u32[]{:S(2)}) copy-start(s16[144,128]{1,0:T(8,128)(2,1)S(1)} %collective-permute-done.7.refs_5_) | copy-start | bytes 110596
  105.9 1.3 copy-start.9
  (1 other events, 0.6 us)
